TPU v7x, 256 devices: a whole 4x4x8 slice. The times are simulated.
256 devices in a mesh: dp: 4 (over z_lo), pipe: 4 (over y), tensor: 16 (over z_hi, x, core).
Axes of the slice: x: 4, y: 4, z: 8 (z_hi: 2, z_lo: 4; z = z_hi * 4 + z_lo), core: 2. Of those that a mesh axis runs over, the one named last changes fastest.
Arguments:
- outgoing: bfloat16 [4, 512, 8192], P('pipe', 'dp', 'tensor'), may hold values from -40 to 40
- stashed_inputs: bfloat16 [4, 512, 8192], P('pipe', 'dp', 'tensor'), may hold values from -1.5 to 1.5
- encoder: bfloat16 [4, 8192, 1024], P('pipe', 'tensor'), may hold values from -0.0625 to 0.0625
- decoder: bfloat16 [4, 1024, 8192], P('pipe', None, ('dp', 'tensor')), may hold values from -0.28125 to 0.28125
- norm_gain: float32 [4, 8192], P('pipe', 'dp'), may hold values from 0.1 to 1.9
- gate_matrix: bfloat16 [4, 8192, 14336], P('pipe', 'dp', 'tensor'), may hold values from -0.0625 to 0.0625
- up_matrix: bfloat16 [4, 8192, 14336], P('pipe', 'dp', 'tensor'), may hold values from -0.0625 to 0.0625
- grad_decoded: bfloat16 [4, 512, 8192], P('pipe', None, ('dp', 'tensor')), may hold values from -1.5 to 1.5
- stashed_codes: bfloat16 [4, 512, 1024], P('pipe', ('dp', 'tensor')), may hold values from -4 to 4
Outputs:
- activated: bfloat16 [4, 512, 14336], P('pipe', 'dp', 'tensor')
- input_grad: bfloat16 [4, 512, 8192], P('pipe', 'dp', 'tensor')
- encoder_grad: float32 [4, 8192, 1024], P('pipe', 'tensor', 'dp')
- decoder_grad: float32 [4, 1024, 8192], P('pipe', None, ('dp', 'tensor'))
All inputs are finite; a program needn't handle non-finite values.
Results may differ from a plain program's by a relative error of at most 0.0082.
Values may be sent and summed in bfloat16 or wider, within the bound.
A program may use at most 64 MiB of HBM per device.

v0:
```python
import jax
import jax.numpy as jnp
from jax import lax
from jax.sharding import PartitionSpec as P

D = 8192


epsilon = 1e-05


def shifted(x, axis, by):
    length = lax.axis_size(axis)
    pairs = [(i, i + by) for i in range(length) if 0 <= i + by < length]
    return lax.ppermute(x, axis, pairs)


def contract_last(left_op, right_op):
    return lax.dot_general(
        left_op, right_op, (((1,), (1,)), ((), ())), preferred_element_type=jnp.float32
    )


def contract_first(left_op, right_op):
    return lax.dot_general(
        left_op, right_op, (((0,), (0,)), ((), ())), preferred_element_type=jnp.float32
    )


def per_device(
    outgoing,
    stashed_inputs,
    encoder,
    decoder,
    norm_gain,
    gate_matrix,
    up_matrix,
    grad_decoded,
    stashed_codes,
):
    local_out = outgoing[0]
    local_enc = encoder[0]
    local_dec = decoder[0]
    local_gain = norm_gain[0]
    local_gate = gate_matrix[0]
    local_up = up_matrix[0]
    local_grad = grad_decoded[0]
    partial_value = jnp.dot(local_out, local_enc, preferred_element_type=jnp.float32)
    code_sum = lax.psum(partial_value, "tensor").astype(jnp.bfloat16)
    arrived = shifted(code_sum, "pipe", 1)
    all_codes = lax.all_gather(arrived, "dp", axis=0, tiled=True)
    decoded = jnp.dot(all_codes, local_dec, preferred_element_type=jnp.float32).astype(jnp.bfloat16)
    rows_all = decoded.shape[0]
    own_rows = rows_all // lax.axis_size("dp")
    own_start = lax.axis_index("dp") * own_rows
    widened = decoded.astype(jnp.float32)
    square_sums = lax.psum(jnp.sum(widened * widened, axis=1), ("dp", "tensor"))
    normed = (
        lax.all_gather(decoded, "tensor", axis=1, tiled=True).astype(jnp.float32)
        * local_gain[None, :]
    ).astype(jnp.bfloat16)
    gate_add = jnp.dot(normed, local_gate, preferred_element_type=jnp.float32)
    up_add = jnp.dot(normed, local_up, preferred_element_type=jnp.float32)
    gate_sum, up_sum = (
        lax.psum_scatter(gate_add, "dp", scatter_dimension=0, tiled=True),
        lax.psum_scatter(up_add, "dp", scatter_dimension=0, tiled=True),
    )
    own_squares = lax.dynamic_slice_in_dim(square_sums, own_start, own_rows, 0)
    inv_rms = lax.rsqrt(own_squares / D + epsilon)[:, None]
    activated = (jax.nn.silu(inv_rms * gate_sum) * (inv_rms * up_sum)).astype(jnp.bfloat16)
    grad_part = lax.psum_scatter(
        contract_last(local_grad, local_dec), ("dp", "tensor"), scatter_dimension=0, tiled=True
    )
    handed = shifted(grad_part.astype(jnp.bfloat16), "pipe", -1)
    returned = lax.all_gather(handed, "tensor", axis=0, tiled=True)
    input_grad = contract_last(returned, local_enc).astype(jnp.bfloat16)
    encoder_part = contract_first(stashed_inputs[0], returned)
    encoder_grad = lax.psum_scatter(encoder_part, "dp", scatter_dimension=1, tiled=True)
    stash_all = lax.all_gather(stashed_codes[0], ("dp", "tensor"), axis=0, tiled=True)
    decoder_grad = contract_first(stash_all, local_grad)
    return (activated[None], input_grad[None], encoder_grad[None], decoder_grad[None])


def solution(mesh):
    placed = (
        P("pipe", "dp", "tensor"),
        P("pipe", "dp", "tensor"),
        P("pipe", "tensor", None),
        P("pipe", None, ("dp", "tensor")),
        P("pipe", "dp"),
        P("pipe", "dp", "tensor"),
        P("pipe", "dp", "tensor"),
        P("pipe", None, ("dp", "tensor")),
        P("pipe", ("dp", "tensor"), None),
    )
    return jax.shard_map(
        per_device,
        mesh=mesh,
        in_specs=placed,
        out_specs=(
            P("pipe", "dp", "tensor"),
            P("pipe", "dp", "tensor"),
            P("pipe", "tensor", "dp"),
            P("pipe", None, ("dp", "tensor")),
        ),
        check_vma=False,
    )
```

profile of v0, /device:TPU:192, one launch (start us, length us, event | category | flops | bytes accessed | tf_op | source)
XLA Modules:
  0.0 717.2 jit_solution(16517025171945548124)
XLA Ops:
  8.1 1.2 copy-done
  9.2 1.2 fusion.7
  10.4 92.0 %all-reduce.1 = bf16[128,1024]{1,0:T(8,128)(2,1)S(1)} all-reduce(f32[128,1024]{1,0:T(8,128)S(1)} %fusion.7), channel_id=1, replica_groups=mesh['dp'=4,'pipe'=4,'tensor'=16] {'tensor'}, use_global_device_ids=true, to_apply=%region_0.0 | all-reduce | flops 131072 | bytes 786432 | tf_op jit(solution)/shard_map/psum | solution.py:49
  102.5 3.5 collective-permute-start
  106.0 3.9 collective-permute-done
  109.8 0.7 copy-done.3
  110.6 1.8 fusion.9
  112.5 30.7 %all-gather.5.cloned.1.call-done = bf16[512,1024]{1,0:T(8,128)(2,1)} async-done(((bf16[128,1024]{1,0:T(8,128)(2,1)}), bf16[512,1024]{1,0:T(8,128)(2,1)}) %all-gather.5.cloned.1.call-update) | async-done | bytes 1048592 | tf_op jit(solution)/shard_map/all_gather | solution.py:51
  143.2 2.4 multiply_reduce_fusion
  145.6 0.7 all-gather.9.cloned.1.call-update
  146.4 328.6 %reduce-scatter.9.cloned.1.call-done = f32[8,1024]{1,0:T(8,128)} async-done(((f32[512,1024]{1,0:T(8,128)}), f32[8,1024]{1,0:T(8,128)}) %reduce-scatter.9.cloned.1.call-update) | async-done | bytes 32784 | tf_op jit(solution)/shard_map/reduce_scatter | solution.py:71
  475.0 0.8 convert_element_type.30
  475.8 1.3 collective-permute-start.1
  477.0 4.3 collective-permute-done.1
  481.4 24.5 %all_gather.14 = bf16[128,1024]{1,0:T(8,128)(2,1)S(1)} all-gather(bf16[8,1024]{1,0:T(8,128)(2,1)S(1)} %collective-permute-done.1), channel_id=1, replica_groups=mesh['dp'=4,'pipe'=4,'tensor'=16] {'tensor'}, dimensions={0}, use_global_device_ids=true | all-gather | bytes 278528 | tf_op jit(solution)/shard_map/all_gather | solution.py:75
  505.9 1.8 convolution_bitcast_fusion
  507.7 6.4 fusion.2
  514.2 6.3 fusion
  520.6 181.4 %psum.15 = f32[512]{0:T(512)S(1)} all-reduce(f32[512]{0:T(512)S(1)} %get-tuple-element.8), channel_id=1, replica_groups=mesh['dp'=4,'pipe'=4,'tensor'=16] {'dp','tensor'}, use_global_device_ids=true, to_apply=%region_2.0 | all-reduce | flops 512 | bytes 4096 | tf_op jit(solution)/shard_map/psum | solution.py:57
  702.0 0.1 add_rsqrt_fusion
  702.1 2.5 convolution_bitcast_fusion.1
  704.6 1.1 fusion.4
  705.7 2.0 copy.13
  707.7 2.1 fusion.12
  (28 shorter events, 0.4 us)
Async XLA Ops:
  8.0 1.2 copy-start
  8.0 102.6 %copy-start.1 = (bf16[1,1024,128]{2,1,0:T(8,128)(2,1)S(1)}, bf16[1,1024,128]{2,1,0:T(8,128)(2,1)}, u32[]{:S(2)}) copy-start(bf16[1,1024,128]{2,1,0:T(8,128)(2,1)} %param.12) | copy-start | bytes 786436
  8.0 102.6 %copy-start.2 = (bf16[1,512,128]{2,1,0:T(8,128)(2,1)S(1)}, bf16[1,512,128]{2,1,0:T(8,128)(2,1)}, u32[]{:S(2)}) copy-start(bf16[1,512,128]{2,1,0:T(8,128)(2,1)} %param.16) | copy-start | bytes 393220
  8.0 135.2 %all-gather.5.cloned.1.call-start = ((), (), s32[]{:S(2)}) async-start(), calls=%async_computation.4 | async-start | bytes 1310720 | tf_op jit(solution)/shard_map/all_gather | solution.py:51
  102.5 7.4 %collective-permute-start = (bf16[128,1024]{1,0:T(8,128)(2,1)S(1)}, bf16[128,1024]{1,0:T(8,128)(2,1)S(1)}, u32[]{:S(2)}, u32[]{:S(2)}) collective-permute-start(bf16[128,1024]{1,0:T(8,128)(2,1)S(1)} %all-reduce.1), channel_id=1, source_target_pairs={{0,16},{16,32},{32,48},{1,17},{17,33},{33,49},{2,18},{18,34},{34,5... | collective-permute-start | bytes 786440 | tf_op jit(solution)/shard_map/ppermute | solution.py:15
  109.8 0.7 copy-start.3
  110.5 364.5 %reduce-scatter.9.cloned.1.call-start = ((), (), s32[]{:S(2)}) async-start(), calls=%async_computation.8 | async-start | bytes 2129920 | tf_op jit(solution)/shard_map/reduce_scatter | solution.py:71
  112.4 393.5 %copy-start.4 = (bf16[1,128,512]{2,1,0:T(8,128)(2,1)S(1)}, bf16[1,128,512]{2,1,0:T(8,128)(2,1)}, u32[]{:S(2)}) copy-start(bf16[1,128,512]{2,1,0:T(8,128)(2,1)} %param.10) | copy-start | bytes 393220
  112.4 395.3 %all-gather.7.cloned.1.call-start = ((), (), s32[]{:S(2)}) async-start(), calls=%async_computation.5 | async-start | bytes 2228224 | tf_op jit(solution)/shard_map/all_gather | solution.py:59
  145.6 556.5 %all-gather.9.cloned.1.call-start = ((), (), s32[]{:S(2)}) async-start(), calls=%async_computation.10 | async-start | bytes 1064960 | tf_op jit(solution)/shard_map/all_gather | solution.py:79
  146.3 559.4 %reduce-scatter.11.cloned.1.call-start = ((), (), s32[]{:S(2)}) async-start(), calls=%async_computation.9 | async-start | bytes 2621440 | tf_op jit(solution)/shard_map/reduce_scatter | solution.py:78
  475.8 5.6 collective-permute-start.1
  505.8 1.9 copy-start.5
  507.7 200.1 %reduce-scatter.5.cloned.1.call-start = ((), (), s32[]{:S(2)}) async-start(), calls=%async_computation.6 | async-start | bytes 2293760 | tf_op jit(solution)/shard_map/reduce_scatter | solution.py:65
  514.1 193.6 %reduce-scatter.7.cloned.1.call-start = ((), (), s32[]{:S(2)}) async-start(), calls=%async_computation.7 | async-start | bytes 2293760 | tf_op jit(solution)/shard_map/reduce_scatter | solution.py:66
Sparse Core Ops, SparseCore 0:
  110.7 32.4 all-gather.4
  146.5 60.4 all-gather.6
  208.8 111.0 all-gather.8
  507.8 46.2 reduce-scatter.10
  556.5 44.0 reduce-scatter.4
  603.0 44.3 reduce-scatter.6
Sparse Core Ops, SparseCore 1:
  113.5 361.4 reduce-scatter.8
where the time goes:
time: 718 us; the launch traced here: 717 us
  waiting for transfers between devices  368 us (51%)
  blocking collectives  298 us (42%)
  matrix products  23.4 us (3%)
  between operations  15.7 us (2%)
    reduce_scatter x1, waiting for transfers between devices, per_device(): lax.psum_scatter(contract_last(local_grad, local_dec), ('dp', 'tensor'),...  329 us
    psum x1, blocking collectives, per_device(): square_sums = lax.psum(jnp.sum(widened * widened, axis=1), ('dp', 'tensor'))  181 us
    psum x1, blocking collectives, per_device(): code_sum = lax.psum(partial_value, 'tensor').astype(jnp.bfloat16)  92 us
    all_gather x1, waiting for transfers between devices, per_device(): all_codes = lax.all_gather(arrived, 'dp', axis=0, tiled=True)  30.7 us
    all_gather x1, blocking collectives, per_device(): returned = lax.all_gather(handed, 'tensor', axis=0, tiled=True)  24.5 us
  transfers between devices with their start and end apart: 9, of which 4 were waited for; matrix products, arithmetic and copies ran while one was open for 4% of the time, Pallas kernels for 0%

commit v1 on v0

v1 whole, which is shorter than its diff:
```python
import jax
import jax.numpy as jnp
from jax import lax
from jax.experimental import pallas as pl
from jax.experimental.pallas import tpu as pltpu
from jax.sharding import PartitionSpec as P

D = 8192
epsilon = 1e-05
MESH = pl.DeviceIdType.MESH
F32 = jnp.float32
BF16 = jnp.bfloat16

LAST = (((1,), (1,)), ((), ()))
FIRST = (((0,), (0,)), ((), ()))


def kernel(
    out_h,
    stin_h,
    enc_h,
    dec_h,
    gain_h,
    gate_h,
    up_h,
    grad_h,
    stc_v,
    act_o,
    ing_o,
    encg_o,
    decg_o,
    out_v,
    enc_v,
    gain_v,
    grad_v,
    stin_v,
    wgu,
    w_all,
    q_send,
    q_recv,
    q_own,
    x_recv,
    r_own,
    z_recv,
    code_sh,
    code,
    blk,
    blk_r,
    st_sh,
    st,
    ga,
    pb,
    pb_r,
    cg_sh,
    ret,
    normed,
    acc,
    gu_s,
    gu_r,
    gu_own,
    ssq,
    ssq_r,
    local_sem,
    wload_sem,
    s_core,
    r_core,
    s_x,
    r_x,
    s_z,
    r_z,
    s_gu,
    r_gu,
):
    dp = lax.axis_index("dp")
    y = lax.axis_index("pipe")
    t = lax.axis_index("tensor")
    zh = t // 8
    x = (t // 2) % 4
    c = t % 2
    z = zh * 4 + dp

    def dev(z_, y_, x_, c_):
        return (z_ % 4, y_, (z_ // 4) * 8 + x_ * 2 + c_)

    sib = dev(z, y, x, 1 - c)
    xs = [(x + k) % 4 for k in range(4)]
    xdev = [dev(z, y, v, c) for v in xs]
    zdev = [dev((z + k) % 8, y, x, c) for k in range(8)]
    updev = [dev((z + k) % 8, (y + 1) % 4, x, c) for k in range(8)]
    downdev = [dev((z + k) % 8, (y + 3) % 4, x, c) for k in range(8)]
    far = [dev((z + 4) % 8, y, v, c) for v in xs]
    dpdev = [((dp + k) % 4, y, t) for k in range(4)]

    def half(c_):
        return pl.ds(pl.multiple_of(c_ * 512, 512), 512)

    own_half = half(c)
    own_lane = pl.ds(pl.multiple_of(c * 128, 128), 128)
    slab = pl.ds(pl.multiple_of((dp * 2 + zh) * 16, 16), 16)

    pending = []

    def send(src, dst, ss, rs, to):
        cp = pltpu.make_async_remote_copy(
            src_ref=src, dst_ref=dst, send_sem=ss, recv_sem=rs, device_id=to, device_id_type=MESH
        )
        cp.start()
        pending.append(cp)
        return cp

    def local(src, dst, sem):
        cp = pltpu.make_async_copy(src, dst, sem)
        cp.start()
        return cp

    l_out = local(out_h.at[0], out_v, local_sem.at[0])
    l_enc = local(enc_h.at[0], enc_v, local_sem.at[1])
    own_w = w_all.at[zh * 4 + x, :, own_lane]
    l_dec = local(dec_h.at[0], own_w, local_sem.at[2])
    own_slot = pl.ds(pl.multiple_of((zh * 4 + x) * 128, 128), 128)
    own_rows = pl.ds(pl.multiple_of(x * 32 + zh * 16, 16), 16)
    l_ga = local(grad_h.at[:, own_rows, :], ga.at[c, :, :, own_slot], local_sem.at[3])
    l_grad = local(grad_h, grad_v, local_sem.at[4])
    l_gain = local(gain_h, gain_v, local_sem.at[5])
    l_stin = local(stin_h.at[0], stin_v.at[dp], local_sem.at[6])
    l_gu = []
    for n in range(7):
        cols = pl.ds(n * 128, 128)
        l_gu.append(local(gate_h.at[0, :, cols], wgu.at[n, :, pl.ds(0, 128)], wload_sem.at[2 * n]))
        l_gu.append(local(up_h.at[0, :, cols], wgu.at[n, :, pl.ds(128, 128)], wload_sem.at[2 * n + 1]))

    barrier = pltpu.get_barrier_semaphore()
    peers = [sib] + xdev[1:] + zdev[1:] + updev + downdev + far[1:]
    for p in peers:
        pl.semaphore_signal(barrier, inc=1, device_id=p, device_id_type=MESH)
    pl.semaphore_wait(barrier, len(peers))

    wz = send(dec_h.at[0], own_w, s_z.at[0], r_z.at[0], zdev[4])
    ga_in = []
    for k in range(4):
        for h in range(2):
            if k == 0 and h == 0:
                continue
            zh_to = (zh + h) % 2
            rows = pl.ds(pl.multiple_of(xs[k] * 32 + zh_to * 16, 16), 16)
            to = far[k] if h else xdev[k]
            i = k * 2 + h
            ga_in.append(
                send(grad_h.at[:, rows, :], ga.at[c, :, :, own_slot], s_x.at[i], r_x.at[i], to)
            )

    l_out.wait()
    l_enc.wait()
    q_send[...] = jnp.dot(out_v[...], enc_v[:, half(1 - c)], preferred_element_type=F32)
    qc = send(q_send, q_recv, s_core.at[0], r_core.at[0], sib)
    stc = stc_v[0].astype(F32)
    blk[...] = jnp.concatenate([stc[:, :512], stc[:, 512:]], axis=0).astype(BF16)
    bc = send(blk, blk_r, s_core.at[1], r_core.at[1], sib)
    q_own[...] = jnp.dot(out_v[...], enc_v[:, own_half], preferred_element_type=F32)
    qc.wait_recv()
    q_own[...] += q_recv[...]
    xr = []
    for k in range(1, 4):
        rows = pl.ds(pl.multiple_of(xs[k] * 32, 32), 32)
        xr.append(send(q_own.at[rows, :], x_recv.at[k - 1], s_x.at[7 + k], r_x.at[7 + k], xdev[k]))
    wx = [send(dec_h.at[0], own_w, s_x.at[10 + k], r_x.at[10 + k], xdev[k]) for k in range(1, 4)]
    wc = [send(dec_h.at[0], own_w, s_core.at[2], r_core.at[2], sib)]

    bc.wait_recv()
    a = blk[...].astype(F32)
    b = blk_r[...].astype(F32)
    mine = jnp.where(c == 0, a[:8], a[8:])
    other = jnp.where(c == 0, b[:8], b[8:])
    first = jnp.where(c == 0, mine, other)
    second = jnp.where(c == 0, other, mine)
    st_val = jnp.concatenate([first, second], axis=0).astype(BF16)
    st_sh[...] = st_val
    st[x, slab, own_half] = st_val

    for cp in xr:
        cp.wait_recv()
    r_own[...] = (
        q_own[pl.ds(pl.multiple_of(x * 32, 32), 32), :] + x_recv[0] + x_recv[1] + x_recv[2]
    )
    zr = send(
        r_own.at[pl.ds(pl.multiple_of((1 - zh) * 16, 16), 16), :],
        z_recv,
        s_z.at[1],
        r_z.at[1],
        zdev[4],
    )
    zr.wait_recv()
    code_val = (r_own[pl.ds(pl.multiple_of(zh * 16, 16), 16), :] + z_recv[...]).astype(BF16)
    code_sh[...] = jnp.where(y == 3, jnp.zeros_like(code_val), code_val)
    cz = [
        send(code_sh, code.at[x, slab, own_half], s_z.at[2 + k], r_z.at[2 + k], updev[k])
        for k in range(8)
    ]
    sz = [
        send(st_sh, st.at[x, slab, own_half], s_z.at[10 + k], r_z.at[10 + k], zdev[k])
        for k in range(1, 8)
    ]
    si = [
        send(stin_h.at[0], stin_v.at[dp], s_z.at[17 + k], r_z.at[17 + k], dpdev[k])
        for k in range(1, 4)
    ]

    wz.wait_recv()
    far_w = w_all.at[(1 - zh) * 4 + x, :, own_lane]
    wx2 = [send(far_w, far_w, s_x.at[13 + k], r_x.at[13 + k], xdev[k]) for k in range(1, 4)]
    wc.append(send(far_w, far_w, s_core.at[3], r_core.at[3], sib))

    for cp in ga_in:
        cp.wait_recv()
    l_ga.wait()
    gac = send(ga.at[c], ga.at[c], s_core.at[10], r_core.at[10], sib)

    def gather_x(buf, base):
        src = buf.at[x, :, own_half]
        return [send(src, src, s_x.at[base + k], r_x.at[base + k], xdev[k]) for k in range(1, 4)]

    def to_sibling(buf, slot, i):
        src = buf.at[slot, :, own_half]
        return send(src, src, s_core.at[i], r_core.at[i], sib)

    for cp in cz:
        cp.wait_recv()
    cc = [to_sibling(code, x, 11)]
    cx = gather_x(code, 16)
    for cp in sz:
        cp.wait_recv()
    sc = [to_sibling(st, x, 15)]
    sx = gather_x(st, 19)

    for k in range(1, 4):
        wx[k - 1].wait_recv()
        ref = w_all.at[zh * 4 + xs[4 - k], :, own_lane]
        wc.append(send(ref, ref, s_core.at[3 + k], r_core.at[3 + k], sib))
    for k in range(1, 4):
        cx[k - 1].wait_recv()
        cc.append(to_sibling(code, xs[4 - k], 11 + k))
    for k in range(1, 4):
        wx2[k - 1].wait_recv()
        ref = w_all.at[(1 - zh) * 4 + xs[4 - k], :, own_lane]
        wc.append(send(ref, ref, s_core.at[6 + k], r_core.at[6 + k], sib))
    for cp in wc:
        cp.wait_recv()

    gac.wait_recv()
    l_dec.wait()
    pb[...] = jnp.zeros_like(pb)

    def back(j, carry):
        lanes = pl.ds(pl.multiple_of(j * 128, 128), 128)
        g = jnp.concatenate(
            [ga[0, :, :, lanes].reshape(64, 128), ga[1, :, :, lanes].reshape(64, 128)], axis=1
        )
        part = lax.dot_general(g, w_all[j, own_half, :], LAST, preferred_element_type=F32)
        pb[...] += part.reshape(4, 16, 512)
        return carry

    lax.fori_loop(0, 8, back, 0)
    pr = [
        send(pb.at[(dp + k) % 4], pb_r.at[k - 1], s_z.at[20 + k], r_z.at[20 + k], dpdev[k])
        for k in range(1, 4)
    ]

    l_gain.wait()
    for cp in l_gu:
        cp.wait()
    lane_id = lax.broadcasted_iota(jnp.int32, (128, 128), 1)
    ssq[...] = jnp.zeros_like(ssq)
    gus = []
    own_m = pl.ds(pl.multiple_of(dp * 32, 32), 32)

    def group(k):
        slot = xs[(4 - k) % 4]
        cc[k].wait_recv()
        acc[...] = jnp.zeros_like(acc)

        def decode(j, carry):
            dec = jnp.dot(code[slot], w_all[j], preferred_element_type=F32)
            dec = dec.astype(BF16).astype(F32)
            cols = pl.ds(pl.multiple_of(j * 256, 256), 256)
            normed[:, cols] = (dec * gain_v[:, cols]).astype(BF16)
            sq = dec * dec
            acc[:, 0:128] += sq[:, :128] + sq[:, 128:]
            return carry

        lax.fori_loop(0, 8, decode, 0)
        total = jnp.sum(acc[:, 0:128], axis=1, keepdims=True)
        ssq[...] += jnp.where(lane_id == k, total, 0.0).reshape(4, 32, 128)

        def project(n, carry):
            v = jnp.dot(normed[...], wgu[n], preferred_element_type=F32)
            acc[...] = v
            gu_s[k, :, n] = v.astype(BF16).reshape(4, 32, 256)
            gu_own[k, n] = acc[own_m, :]
            return carry

        lax.fori_loop(0, 7, project, 0)
        for q in range(1, 4):
            gus.append(
                send(
                    gu_s.at[k, (dp + q) % 4],
                    gu_r.at[k, q - 1],
                    s_gu.at[k * 3 + q - 1],
                    r_gu.at[k * 3 + q - 1],
                    dpdev[q],
                )
            )

    group(0)
    for cp in pr:
        cp.wait_recv()
    cg = (pb[dp] + pb_r[0] + pb_r[1] + pb_r[2]).astype(BF16)
    cg_sh[...] = jnp.where(y == 0, jnp.zeros_like(cg), cg)
    rz = [
        send(cg_sh, ret.at[x, slab, own_half], s_z.at[24 + k], r_z.at[24 + k], downdev[k])
        for k in range(8)
    ]
    group(1)
    group(2)
    group(3)
    sq_in = [
        send(ssq.at[(dp + q) % 4], ssq_r.at[q - 1], s_gu.at[11 + q], r_gu.at[11 + q], dpdev[q])
        for q in range(1, 4)
    ]

    for cp in rz:
        cp.wait_recv()
    rc = [to_sibling(ret, x, 19)]
    rx = gather_x(ret, 22)

    for k in range(1, 4):
        sx[k - 1].wait_recv()
        sc.append(to_sibling(st, xs[4 - k], 15 + k))
    l_grad.wait()
    for cp in sc:
        cp.wait_recv()
    grads = grad_v[...].reshape(4, 2, 4, 16, 128)
    perm = jnp.concatenate([grads[:, :, v].reshape(128, 128) for v in range(4)], axis=0)
    for h in range(4):
        cols = pl.ds(h * 256, 256)
        lhs = st[:, :, cols].reshape(512, 256)
        decg_o[0, cols, :] = lax.dot_general(lhs, perm, FIRST, preferred_element_type=F32)

    for k in range(1, 4):
        rx[k - 1].wait_recv()
        rc.append(to_sibling(ret, xs[4 - k], 19 + k))
    for cp in rc:
        cp.wait_recv()
    l_stin.wait()
    for cp in si:
        cp.wait_recv()
    for v in range(4):
        own_ret = ret[v, own_m, :]
        ing_o[0, pl.ds(v * 32, 32), :] = lax.dot_general(
            own_ret, enc_v[...], LAST, preferred_element_type=F32
        ).astype(BF16)
    rhs = ret[:, :, pl.ds(pl.multiple_of(dp * 256, 256), 256)].reshape(512, 256)
    for h in range(2):
        cols = pl.ds(h * 256, 256)
        lhs = jnp.concatenate(
            [stin_v[:, pl.ds(v * 32, 32), cols].reshape(128, 256) for v in range(4)], axis=0
        )
        encg_o[0, cols, :] = lax.dot_general(lhs, rhs, FIRST, preferred_element_type=F32)

    for cp in sq_in:
        cp.wait_recv()
    total = ssq[dp] + ssq_r[0] + ssq_r[1] + ssq_r[2]
    inv_all = lax.rsqrt(total / D + epsilon)
    for k in range(4):
        for q in range(3):
            gus[k * 3 + q].wait_recv()
        inv = inv_all[:, k : k + 1]
        rows = pl.ds(pl.multiple_of(xs[(4 - k) % 4] * 32, 32), 32)
        for n in range(7):
            s = (
                gu_own[k, n]
                + gu_r[k, 0, n].astype(F32)
                + gu_r[k, 1, n].astype(F32)
                + gu_r[k, 2, n].astype(F32)
            ) * inv
            gate = s[:, :128]
            act = gate / (1.0 + jnp.exp(-gate)) * s[:, 128:]
            act_o[0, rows, pl.ds(n * 128, 128)] = act.astype(BF16)

    for cp in pending:
        cp.wait_send()


def per_device(
    outgoing,
    stashed_inputs,
    encoder,
    decoder,
    norm_gain,
    gate_matrix,
    up_matrix,
    grad_decoded,
    stashed_codes,
):
    grad = grad_decoded.reshape(4, 128, 128)
    anywhere = pl.BlockSpec(memory_space=pl.ANY)
    vmem = pl.BlockSpec(memory_space=pltpu.VMEM)
    V = pltpu.VMEM
    DMA = pltpu.SemaphoreType.DMA
    return pl.pallas_call(
        kernel,
        name="section",
        out_shape=(
            jax.ShapeDtypeStruct((1, 128, 896), BF16),
            jax.ShapeDtypeStruct((1, 128, 512), BF16),
            jax.ShapeDtypeStruct((1, 512, 256), F32),
            jax.ShapeDtypeStruct((1, 1024, 128), F32),
        ),
        in_specs=[anywhere] * 8 + [vmem],
        out_specs=(vmem,) * 4,
        scratch_shapes=[
            V((128, 512), BF16),
            V((512, 1024), BF16),
            V((1, 2048), F32),
            V((4, 128, 128), BF16),
            V((4, 128, 512), BF16),
            V((7, 2048, 256), BF16),
            V((8, 1024, 256), BF16),
            V((128, 512), F32),
            V((128, 512), F32),
            V((128, 512), F32),
            V((3, 32, 512), F32),
            V((32, 512), F32),
            V((16, 512), F32),
            V((16, 512), BF16),
            V((4, 128, 1024), BF16),
            V((16, 512), BF16),
            V((16, 512), BF16),
            V((16, 512), BF16),
            V((4, 128, 1024), BF16),
            V((2, 4, 16, 1024), BF16),
            V((4, 16, 512), F32),
            V((3, 16, 512), F32),
            V((16, 512), BF16),
            V((4, 128, 1024), BF16),
            V((128, 2048), BF16),
            V((128, 256), F32),
            V((4, 4, 7, 32, 256), BF16),
            V((4, 3, 7, 32, 256), BF16),
            V((4, 7, 32, 256), F32),
            V((4, 32, 128), F32),
            V((3, 32, 128), F32),
            DMA((7,)),
            DMA((14,)),
            DMA((23,)),
            DMA((23,)),
            DMA((26,)),
            DMA((26,)),
            DMA((32,)),
            DMA((32,)),
            DMA((15,)),
            DMA((15,)),
        ],
        compiler_params=pltpu.CompilerParams(
            collective_id=0, has_side_effects=True, vmem_limit_bytes=60 * 2**20
        ),
    )(
        outgoing,
        stashed_inputs,
        encoder,
        decoder,
        norm_gain,
        gate_matrix,
        up_matrix,
        grad,
        stashed_codes,
    )


def solution(mesh):
    placed = (
        P("pipe", "dp", "tensor"),
        P("pipe", "dp", "tensor"),
        P("pipe", "tensor", None),
        P("pipe", None, ("dp", "tensor")),
        P("pipe", "dp"),
        P("pipe", "dp", "tensor"),
        P("pipe", "dp", "tensor"),
        P("pipe", None, ("dp", "tensor")),
        P("pipe", ("dp", "tensor"), None),
    )
    return jax.shard_map(
        per_device,
        mesh=mesh,
        in_specs=placed,
        out_specs=(
            P("pipe", "dp", "tensor"),
            P("pipe", "dp", "tensor"),
            P("pipe", "tensor", "dp"),
            P("pipe", None, ("dp", "tensor")),
        ),
        check_vma=False,
    )
```

time: 718 us -> 115 us (0.16)
  the two profiles are of different devices: /device:TPU:192 before, /device:TPU:1 now
where the time goes in v1:
time: 115 us
  Pallas kernels  107 us (93%)
  local copies, waits for them, and re-layouts  6.95 us (6%)
    pallas_call x1, Pallas kernels, per_device(): pl.pallas_call(kernel, name='section', out_shape=(jax.ShapeDtypeStruct((1...  107 us
    unnamed x4, local copies, waits for them, and re-layouts  6.95 us

profile of v1, /device:TPU:1, one launch (start us, length us, event | category | flops | bytes accessed | tf_op | source)
XLA Modules:
  0.0 114.8 jit_solution(3709753564410984084)
XLA Ops:
  0.6 107.2 %section.1 = (bf16[1,128,896]{2,1,0:T(8,128)(2,1)}, bf16[1,128,512]{2,1,0:T(8,128)(2,1)}, f32[1,512,256]{2,1,0:T(8,128)}, f32[1,1024,128]{2,1,0:T(8,128)}) custom-call(bf16[1,128,512]{2,1,0:T(8,128)(2,1)} %out_h.1, bf16[1,128,512]{2,1,0:T(8,128)(2,1)} %stin_h.1, bf16[1,512,1024]{2,1,0:T(8,128)(2,1)} %enc_h.1, bf16[1,1024,128]{2,1,0:T(8,128)(2,1)} %dec_h.1, ...), custom_call_target="tpu_custom_call" | custom-call | tf_op jit(solution)/shard_map/section/pallas_call | solution.py:409
  107.8 1.6 %copy.17 = bf16[1,128,896]{2,1,0:T(8,128)(2,1)} copy(bf16[1,128,896]{2,1,0:T(8,128)(2,1)} %get-tuple-element.8) | data formatting | bytes 458752
  109.5 1.6 %copy.18 = bf16[1,128,512]{2,1,0:T(8,128)(2,1)} copy(bf16[1,128,512]{2,1,0:T(8,128)(2,1)} %get-tuple-element.9) | data formatting | bytes 262144
  111.0 1.9 %copy.19 = f32[1,512,256]{2,1,0:T(8,128)} copy(f32[1,512,256]{2,1,0:T(8,128)} %get-tuple-element.10) | data formatting | bytes 1048576
  112.9 1.9 %copy.20 = f32[1,1024,128]{2,1,0:T(8,128)} copy(f32[1,1024,128]{2,1,0:T(8,128)} %get-tuple-element.11) | data formatting | bytes 1048576

commit v2 on v1

--- a/solution.py
+++ b/solution.py
@@ -58,6 +58,7 @@
     gu_s,
     gu_r,
     gu_own,
+    gu_far,
     ssq,
     ssq_r,
     local_sem,
@@ -135,7 +136,18 @@
         pl.semaphore_signal(barrier, inc=1, device_id=p, device_id_type=MESH)
     pl.semaphore_wait(barrier, len(peers))
 
-    wz = send(dec_h.at[0], own_w, s_z.at[0], r_z.at[0], zdev[4])
+    top, bottom = pl.ds(0, 512), pl.ds(512, 512)
+    halves = (top, bottom)
+
+    def w_part(j, rows):
+        return w_all.at[j, rows, own_lane]
+
+    near_j = zh * 4
+    far_j = (1 - zh) * 4
+    wz = [
+        send(dec_h.at[0, rows, :], w_part(near_j + x, rows), s_z.at[i], r_z.at[i], zdev[4])
+        for i, rows in ((0, top), (32, bottom))
+    ]
     ga_in = []
     for k in range(4):
         for h in range(2):
@@ -163,7 +175,13 @@
     for k in range(1, 4):
         rows = pl.ds(pl.multiple_of(xs[k] * 32, 32), 32)
         xr.append(send(q_own.at[rows, :], x_recv.at[k - 1], s_x.at[7 + k], r_x.at[7 + k], xdev[k]))
-    wx = [send(dec_h.at[0], own_w, s_x.at[10 + k], r_x.at[10 + k], xdev[k]) for k in range(1, 4)]
+    wx = {}
+    for k, h in ((1, 0), (3, 1), (1, 1), (3, 0)):
+        i = 11 + (k // 2) * 2 + h
+        rows = halves[h]
+        wx[k, h] = send(
+            dec_h.at[0, rows, :], w_part(near_j + x, rows), s_x.at[i], r_x.at[i], xdev[k]
+        )
     wc = [send(dec_h.at[0], own_w, s_core.at[2], r_core.at[2], sib)]
 
     bc.wait_recv()
@@ -189,6 +207,29 @@
         r_z.at[1],
         zdev[4],
     )
+    wf = {}
+
+    def far_out(h):
+        wz[h].wait_recv()
+        src = w_part(far_j + x, halves[h])
+        for k in (1, 3):
+            i = 15 + (k // 2) * 2 + h
+            wf[k, h] = send(src, src, s_x.at[i], r_x.at[i], xdev[k])
+
+    def pass_on(group, j, i):
+        group[1, 0].wait_recv()
+        src = w_part(j + xs[3], top)
+        right = send(src, src, s_x.at[i], r_x.at[i], xdev[1])
+        group[3, 1].wait_recv()
+        src = w_part(j + xs[1], bottom)
+        left = send(src, src, s_x.at[i + 1], r_x.at[i + 1], xdev[3])
+        return right, left
+
+    def core_out(j, i):
+        src = w_all.at[j, :, own_lane]
+        wc.append(send(src, src, s_core.at[i], r_core.at[i], sib))
+
+    far_out(0)
     zr.wait_recv()
     code_val = (r_own[pl.ds(pl.multiple_of(zh * 16, 16), 16), :] + z_recv[...]).astype(BF16)
     code_sh[...] = jnp.where(y == 3, jnp.zeros_like(code_val), code_val)
@@ -196,6 +237,8 @@
         send(code_sh, code.at[x, slab, own_half], s_z.at[2 + k], r_z.at[2 + k], updev[k])
         for k in range(8)
     ]
+    far_out(1)
+    wx_fwd = pass_on(wx, near_j, 19)
     sz = [
         send(st_sh, st.at[x, slab, own_half], s_z.at[10 + k], r_z.at[10 + k], zdev[k])
         for k in range(1, 8)
@@ -204,16 +247,16 @@
         send(stin_h.at[0], stin_v.at[dp], s_z.at[17 + k], r_z.at[17 + k], dpdev[k])
         for k in range(1, 4)
     ]
-
-    wz.wait_recv()
-    far_w = w_all.at[(1 - zh) * 4 + x, :, own_lane]
-    wx2 = [send(far_w, far_w, s_x.at[13 + k], r_x.at[13 + k], xdev[k]) for k in range(1, 4)]
-    wc.append(send(far_w, far_w, s_core.at[3], r_core.at[3], sib))
-
+    core_out(far_j + x, 3)
     for cp in ga_in:
         cp.wait_recv()
     l_ga.wait()
     gac = send(ga.at[c], ga.at[c], s_core.at[10], r_core.at[10], sib)
+    wx[1, 1].wait_recv()
+    core_out(near_j + xs[3], 4)
+    wx[3, 0].wait_recv()
+    core_out(near_j + xs[1], 5)
+    wf_fwd = pass_on(wf, far_j, 21)
 
     def gather_x(buf, base):
         src = buf.at[x, :, own_half]
@@ -226,23 +269,17 @@
     for cp in cz:
         cp.wait_recv()
     cc = [to_sibling(code, x, 11)]
-    cx = gather_x(code, 16)
-    for cp in sz:
-        cp.wait_recv()
-    sc = [to_sibling(st, x, 15)]
-    sx = gather_x(st, 19)
-
-    for k in range(1, 4):
-        wx[k - 1].wait_recv()
-        ref = w_all.at[zh * 4 + xs[4 - k], :, own_lane]
-        wc.append(send(ref, ref, s_core.at[3 + k], r_core.at[3 + k], sib))
-    for k in range(1, 4):
-        cx[k - 1].wait_recv()
-        cc.append(to_sibling(code, xs[4 - k], 11 + k))
-    for k in range(1, 4):
-        wx2[k - 1].wait_recv()
-        ref = w_all.at[(1 - zh) * 4 + xs[4 - k], :, own_lane]
-        wc.append(send(ref, ref, s_core.at[6 + k], r_core.at[6 + k], sib))
+    cx = gather_x(code, 22)
+    for cp in wx_fwd:
+        cp.wait_recv()
+    core_out(near_j + xs[2], 6)
+    wf[1, 1].wait_recv()
+    core_out(far_j + xs[3], 7)
+    wf[3, 0].wait_recv()
+    core_out(far_j + xs[1], 8)
+    for cp in wf_fwd:
+        cp.wait_recv()
+    core_out(far_j + xs[2], 9)
     for cp in wc:
         cp.wait_recv()
 
@@ -270,8 +307,46 @@
         cp.wait()
     lane_id = lax.broadcasted_iota(jnp.int32, (128, 128), 1)
     ssq[...] = jnp.zeros_like(ssq)
-    gus = []
     own_m = pl.ds(pl.multiple_of(dp * 32, 32), 32)
+
+    is_end = ((dp + 1) // 2 + 1) % 2
+    near = 1 + dp % 2
+    other_dp = (dp * 3 + 2) % 5
+    opp = 3 * (1 - dp // 2)
+    third_dp = is_end * near + (1 - is_end) * opp
+    third_slot = 1 + 2 * is_end
+    far_m = pl.ds(pl.multiple_of(opp * 32, 32), 32)
+    parts = ((0, 4), (4, 7))
+
+    def at_dp(v):
+        return (v, y, t)
+
+    def gu_at(buf, k, m, h):
+        return buf.at[k, m, pl.ds(parts[h][0], parts[h][1] - parts[h][0])]
+
+    def r_in(k, h, slot):
+        return r_gu.at[(k * 2 + h) * 4 + slot]
+
+    def third(k, h):
+        return pltpu.make_async_remote_copy(
+            src_ref=gu_at(gu_s, k, opp, h),
+            dst_ref=gu_at(gu_r, k, third_slot, h),
+            send_sem=s_gu.at[(k * 2 + h) * 3 + 2],
+            recv_sem=r_in(k, h, third_slot),
+            device_id=at_dp(third_dp),
+            device_id_type=MESH,
+        )
+
+    def wait_in(k, h, slot):
+        ref = gu_at(gu_r, k, slot, h)
+        pltpu.make_async_remote_copy(
+            src_ref=ref,
+            dst_ref=ref,
+            send_sem=s_gu.at[0],
+            recv_sem=r_in(k, h, slot),
+            device_id=dpdev[1],
+            device_id_type=MESH,
+        ).wait_recv()
 
     def group(k):
         slot = xs[(4 - k) % 4]
@@ -296,21 +371,39 @@
             acc[...] = v
             gu_s[k, :, n] = v.astype(BF16).reshape(4, 32, 256)
             gu_own[k, n] = acc[own_m, :]
+            gu_far[k, n] = acc[far_m, :]
             return carry
 
-        lax.fori_loop(0, 7, project, 0)
-        for q in range(1, 4):
-            gus.append(
-                send(
-                    gu_s.at[k, (dp + q) % 4],
-                    gu_r.at[k, q - 1],
-                    s_gu.at[k * 3 + q - 1],
-                    r_gu.at[k * 3 + q - 1],
-                    dpdev[q],
-                )
+        for h in range(2):
+            lax.fori_loop(parts[h][0], parts[h][1], project, 0)
+            i = (k * 2 + h) * 3
+
+            @pl.when(is_end == 1)
+            def _():
+                third(k, h).start()
+
+            send(gu_at(gu_s, k, near, h), gu_at(gu_r, k, is_end, h), s_gu.at[i], r_in(k, h, is_end), at_dp(near))
+            send(
+                gu_at(gu_s, k, other_dp, h),
+                gu_at(gu_r, k, 2 * is_end, h),
+                s_gu.at[i + 1],
+                r_in(k, h, 2 * is_end),
+                at_dp(other_dp),
             )
 
+    def merge(k):
+        @pl.when(is_end == 0)
+        def _():
+            for h in range(2):
+                wait_in(k, h, 3)
+                n = pl.ds(parts[h][0], parts[h][1] - parts[h][0])
+                gu_s[k, opp, n] = (gu_far[k, n] + gu_r[k, 3, n].astype(F32)).astype(BF16)
+                third(k, h).start()
+
     group(0)
+    for k in range(1, 4):
+        cx[k - 1].wait_recv()
+        cc.append(to_sibling(code, xs[4 - k], 11 + k))
     for cp in pr:
         cp.wait_recv()
     cg = (pb[dp] + pb_r[0] + pb_r[1] + pb_r[2]).astype(BF16)
@@ -320,17 +413,25 @@
         for k in range(8)
     ]
     group(1)
+    merge(0)
+    for cp in sz:
+        cp.wait_recv()
+    sc = [to_sibling(st, x, 15)]
+    sx = gather_x(st, 25)
     group(2)
+    merge(1)
     group(3)
     sq_in = [
-        send(ssq.at[(dp + q) % 4], ssq_r.at[q - 1], s_gu.at[11 + q], r_gu.at[11 + q], dpdev[q])
+        send(ssq.at[(dp + q) % 4], ssq_r.at[q - 1], s_gu.at[23 + q], r_gu.at[31 + q], dpdev[q])
         for q in range(1, 4)
     ]
+    merge(2)
 
     for cp in rz:
         cp.wait_recv()
     rc = [to_sibling(ret, x, 19)]
-    rx = gather_x(ret, 22)
+    rx = gather_x(ret, 28)
+    merge(3)
 
     for k in range(1, 4):
         sx[k - 1].wait_recv()
@@ -371,8 +472,16 @@
     total = ssq[dp] + ssq_r[0] + ssq_r[1] + ssq_r[2]
     inv_all = lax.rsqrt(total / D + epsilon)
     for k in range(4):
-        for q in range(3):
-            gus[k * 3 + q].wait_recv()
+        for h in range(2):
+            wait_in(k, h, 0)
+            wait_in(k, h, 1)
+
+        @pl.when(is_end == 0)
+        def _():
+            for h in range(2):
+                wait_in(k, h, 2)
+            gu_own[k] += gu_r[k, 2].astype(F32)
+
         inv = inv_all[:, k : k + 1]
         rows = pl.ds(pl.multiple_of(xs[(4 - k) % 4] * 32, 32), 32)
         for n in range(7):
@@ -380,7 +489,6 @@
                 gu_own[k, n]
                 + gu_r[k, 0, n].astype(F32)
                 + gu_r[k, 1, n].astype(F32)
-                + gu_r[k, 2, n].astype(F32)
             ) * inv
             gate = s[:, :128]
             act = gate / (1.0 + jnp.exp(-gate)) * s[:, 128:]
@@ -388,6 +496,24 @@
 
     for cp in pending:
         cp.wait_send()
+    for k in range(4):
+        for h in range(2):
+            third(k, h).wait_send()
+
+
+def hand_over(a, b, c, d, a_o, b_o, c_o, d_o, a_v, b_v, c_v, d_v, sem):
+    steps = ((c, c_v, c_o), (d, d_v, d_o), (a, a_v, a_o), (b, b_v, b_o))
+    loads = [pltpu.make_async_copy(src, via, sem.at[i]) for i, (src, via, _) in enumerate(steps)]
+    stores = [
+        pltpu.make_async_copy(via, dst, sem.at[4 + i]) for i, (_, via, dst) in enumerate(steps)
+    ]
+    for cp in loads:
+        cp.start()
+    for load, store in zip(loads, stores):
+        load.wait()
+        store.start()
+    for cp in stores:
+        cp.wait()
 
 
 def per_device(
@@ -406,15 +532,16 @@
     vmem = pl.BlockSpec(memory_space=pltpu.VMEM)
     V = pltpu.VMEM
     DMA = pltpu.SemaphoreType.DMA
-    return pl.pallas_call(
+    shapes = (
+        jax.ShapeDtypeStruct((1, 128, 896), BF16),
+        jax.ShapeDtypeStruct((1, 128, 512), BF16),
+        jax.ShapeDtypeStruct((1, 512, 256), F32),
+        jax.ShapeDtypeStruct((1, 1024, 128), F32),
+    )
+    results = pl.pallas_call(
         kernel,
         name="section",
-        out_shape=(
-            jax.ShapeDtypeStruct((1, 128, 896), BF16),
-            jax.ShapeDtypeStruct((1, 128, 512), BF16),
-            jax.ShapeDtypeStruct((1, 512, 256), F32),
-            jax.ShapeDtypeStruct((1, 1024, 128), F32),
-        ),
+        out_shape=shapes,
         in_specs=[anywhere] * 8 + [vmem],
         out_specs=(vmem,) * 4,
         scratch_shapes=[
@@ -445,7 +572,8 @@
             V((128, 2048), BF16),
             V((128, 256), F32),
             V((4, 4, 7, 32, 256), BF16),
-            V((4, 3, 7, 32, 256), BF16),
+            V((4, 4, 7, 32, 256), BF16),
+            V((4, 7, 32, 256), F32),
             V((4, 7, 32, 256), F32),
             V((4, 32, 128), F32),
             V((3, 32, 128), F32),
@@ -453,12 +581,12 @@
             DMA((14,)),
             DMA((23,)),
             DMA((23,)),
-            DMA((26,)),
-            DMA((26,)),
             DMA((32,)),
             DMA((32,)),
-            DMA((15,)),
-            DMA((15,)),
+            DMA((33,)),
+            DMA((33,)),
+            DMA((27,)),
+            DMA((35,)),
         ],
         compiler_params=pltpu.CompilerParams(
             collective_id=0, has_side_effects=True, vmem_limit_bytes=60 * 2**20
@@ -474,6 +602,15 @@
         grad,
         stashed_codes,
     )
+    return pl.pallas_call(
+        hand_over,
+        name="hand_over",
+        out_shape=shapes,
+        in_specs=[anywhere] * 4,
+        out_specs=(anywhere,) * 4,
+        scratch_shapes=[V(s.shape, s.dtype) for s in shapes] + [DMA((8,))],
+        compiler_params=pltpu.CompilerParams(vmem_limit_bytes=60 * 2**20),
+    )(*results)
 
 
 def solution(mesh):

time: 115 us -> 90.3 us (0.79)
  Pallas kernels: 107 us -> 89.5 us
  local copies, waits for them, and re-layouts: 6.95 us -> 0 us
    pallas_call x1 -> x2, Pallas kernels: 107 us -> 89.5 us  [the longest x1 87.3 us: per_device(): pl.pallas_call(kernel, name='section', out_shape=shapes, in_specs=[anywhe...]
    unnamed x4 -> x0, local copies, waits for them, and re-layouts: 6.95 us -> none
where the time goes in v2:
time: 90.3 us; the launch traced here: 90.1 us
  Pallas kernels  89.5 us (99%)
    pallas_call x1, Pallas kernels, per_device(): pl.pallas_call(kernel, name='section', out_shape=shapes, in_specs=[anywhe...  87.3 us
    pallas_call x1, Pallas kernels, per_device(): pl.pallas_call(hand_over, name='hand_over', out_shape=shapes, in_specs=[a...  2.19 us

profile of v2, /device:TPU:1, one launch (start us, length us, event | category | flops | bytes accessed | tf_op | source)
XLA Modules:
  0.0 90.1 jit_solution(1107006313132459951)
XLA Ops:
  0.6 87.3 %section.1 = (bf16[1,128,896]{2,1,0:T(8,128)(2,1)}, bf16[1,128,512]{2,1,0:T(8,128)(2,1)}, f32[1,512,256]{2,1,0:T(8,128)}, f32[1,1024,128]{2,1,0:T(8,128)}) custom-call(bf16[1,128,512]{2,1,0:T(8,128)(2,1)} %out_h.1, bf16[1,128,512]{2,1,0:T(8,128)(2,1)} %stin_h.1, bf16[1,512,1024]{2,1,0:T(8,128)(2,1)} %enc_h.1, bf16[1,1024,128]{2,1,0:T(8,128)(2,1)} %dec_h.1, ...), custom_call_target="tpu_custom_call" | custom-call | tf_op jit(solution)/shard_map/section/pallas_call | solution.py:541
  87.9 2.2 %hand_over.1 = (bf16[1,128,896]{2,1,0:T(8,128)(2,1)}, bf16[1,128,512]{2,1,0:T(8,128)(2,1)}, f32[1,512,256]{2,1,0:T(8,128)}, f32[1,1024,128]{2,1,0:T(8,128)}) custom-call(bf16[1,128,896]{2,1,0:T(8,128)(2,1)} %get-tuple-element.8.a, bf16[1,128,512]{2,1,0:T(8,128)(2,1)} %get-tuple-element.9.b, f32[1,512,256]{2,1,0:T(8,128)} %get-tuple-element.10.c, ...), custom_call_target="tpu_custom_call" | custom-call | tf_op jit(solution)/shard_map/hand_over/pallas_call | solution.py:605

commit v3 on v2

v3 whole, which is shorter than its diff:
```python
import jax
import jax.numpy as jnp
from jax import lax
from jax.experimental import pallas as pl
from jax.experimental.pallas import tpu as pltpu
from jax.sharding import PartitionSpec as P

D = 8192
epsilon = 1e-05
MESH = pl.DeviceIdType.MESH
F32 = jnp.float32
BF16 = jnp.bfloat16

LAST = (((1,), (1,)), ((), ()))
FIRST = (((0,), (0,)), ((), ()))


def kernel(
    out_h,
    stin_h,
    enc_h,
    dec_h,
    gain_h,
    gate_h,
    up_h,
    grad_h,
    stc_v,
    act_o,
    ing_o,
    encg_o,
    decg_o,
    out_v,
    enc_v,
    gain_v,
    grad_v,
    stin_v,
    wgu,
    w_all,
    q_send,
    q_recv,
    q_own,
    x_recv,
    r_own,
    z_recv,
    code_sh,
    code,
    blk,
    blk_r,
    st_sh,
    st,
    ga,
    pb,
    pb_s,
    pb_r,
    cg_sh,
    ret,
    dec_s,
    dfar,
    normed,
    acc,
    gu_s,
    gu_r,
    gu_own,
    gu_far,
    ssq,
    ssq_r,
    local_sem,
    wload_sem,
    s_core,
    r_core,
    s_x,
    r_x,
    s_z,
    r_z,
    s_gu,
    r_gu,
):
    dp = lax.axis_index("dp")
    y = lax.axis_index("pipe")
    t = lax.axis_index("tensor")
    zh = t // 8
    x = (t // 2) % 4
    c = t % 2
    z = zh * 4 + dp

    def dev(z_, y_, x_, c_):
        return (z_ % 4, y_, (z_ // 4) * 8 + x_ * 2 + c_)

    sib = dev(z, y, x, 1 - c)
    xs = [(x + k) % 4 for k in range(4)]
    xdev = [dev(z, y, v, c) for v in xs]
    zdev = [dev((z + k) % 8, y, x, c) for k in range(8)]
    updev = [dev((z + k) % 8, (y + 1) % 4, x, c) for k in range(8)]
    downdev = [dev((z + k) % 8, (y + 3) % 4, x, c) for k in range(8)]
    dpdev = [((dp + k) % 4, y, t) for k in range(4)]

    def half(c_):
        return pl.ds(pl.multiple_of(c_ * 512, 512), 512)

    own_half = half(c)
    own_lane = pl.ds(pl.multiple_of(c * 128, 128), 128)
    slab = pl.ds(pl.multiple_of((dp * 2 + zh) * 16, 16), 16)

    pending = []

    def send(src, dst, ss, rs, to):
        cp = pltpu.make_async_remote_copy(
            src_ref=src, dst_ref=dst, send_sem=ss, recv_sem=rs, device_id=to, device_id_type=MESH
        )
        cp.start()
        pending.append(cp)
        return cp

    def local(src, dst, sem):
        cp = pltpu.make_async_copy(src, dst, sem)
        cp.start()
        return cp

    barrier = pltpu.get_barrier_semaphore()
    peers = [sib] + xdev[1:] + zdev[1:] + updev + downdev
    for p in peers:
        pl.semaphore_signal(barrier, inc=1, device_id=p, device_id_type=MESH)

    l_out = local(out_h.at[0], out_v, local_sem.at[0])
    l_enc = local(enc_h.at[0], enc_v, local_sem.at[1])
    own_w = w_all.at[x, :, own_lane]
    l_dec = local(dec_h.at[0], own_w, local_sem.at[2])
    own_slot = pl.ds(pl.multiple_of(x * 128, 128), 128)
    own_rows = pl.ds(pl.multiple_of(x * 32, 32), 32)
    l_ga = local(grad_h.at[:, own_rows, :], ga.at[c, :, :, own_slot], local_sem.at[3])
    l_grad = local(grad_h, grad_v, local_sem.at[4])
    l_gain = local(gain_h, gain_v, local_sem.at[5])
    l_stin = local(stin_h.at[0], stin_v.at[dp], local_sem.at[6])
    l_gu = [
        local(gate_h.at[0], wgu.at[0], wload_sem.at[0]),
        local(up_h.at[0], wgu.at[1], wload_sem.at[1]),
    ]

    l_out.wait()
    l_enc.wait()
    q_send[...] = jnp.dot(out_v[...], enc_v[:, half(1 - c)], preferred_element_type=F32)
    q_own[...] = jnp.dot(out_v[...], enc_v[:, own_half], preferred_element_type=F32)
    stc = stc_v[0].astype(F32)
    blk[...] = jnp.concatenate([stc[:, :512], stc[:, 512:]], axis=0).astype(BF16)
    pl.semaphore_wait(barrier, len(peers))
    qc = send(q_send, q_recv, s_core.at[0], r_core.at[0], sib)
    bc = send(blk, blk_r, s_core.at[1], r_core.at[1], sib)

    si = [
        send(stin_h.at[0], stin_v.at[dp], s_z.at[17 + k], r_z.at[17 + k], dpdev[k])
        for k in range(1, 4)
    ]

    qc.wait_recv()
    q_own[...] += q_recv[...]
    xr = []
    for k in range(1, 4):
        rows = pl.ds(pl.multiple_of(xs[k] * 32, 32), 32)
        xr.append(send(q_own.at[rows, :], x_recv.at[k - 1], s_x.at[7 + k], r_x.at[7 + k], xdev[k]))

    halves = (pl.ds(0, 512), pl.ds(512, 512))
    wx = {}
    for k, h in ((1, 0), (3, 1), (1, 1), (3, 0)):
        i = 11 + (k // 2) * 2 + h
        rows = halves[h]
        wx[k, h] = send(
            dec_h.at[0, rows, :], w_all.at[x, rows, own_lane], s_x.at[i], r_x.at[i], xdev[k]
        )
    wc = [send(dec_h.at[0], own_w, s_core.at[2], r_core.at[2], sib)]

    bc.wait_recv()
    a = blk[...].astype(F32)
    b = blk_r[...].astype(F32)
    mine = jnp.where(c == 0, a[:8], a[8:])
    other = jnp.where(c == 0, b[:8], b[8:])
    first = jnp.where(c == 0, mine, other)
    second = jnp.where(c == 0, other, mine)
    st_val = jnp.concatenate([first, second], axis=0).astype(BF16)
    st_sh[...] = st_val
    st[x, slab, own_half] = st_val

    ga_in = []
    for k in range(1, 4):
        rows = pl.ds(pl.multiple_of(xs[k] * 32, 32), 32)
        ga_in.append(
            send(grad_h.at[:, rows, :], ga.at[c, :, :, own_slot], s_x.at[k], r_x.at[k], xdev[k])
        )

    def core_out(slot, i):
        src = w_all.at[slot, :, own_lane]
        wc.append(send(src, src, s_core.at[i], r_core.at[i], sib))

    def gather_x(buf, base):
        src = buf.at[x, :, own_half]
        return [send(src, src, s_x.at[base + k], r_x.at[base + k], xdev[k]) for k in range(1, 4)]

    def to_sibling(buf, slot, i):
        src = buf.at[slot, :, own_half]
        return send(src, src, s_core.at[i], r_core.at[i], sib)

    for cp in xr:
        cp.wait_recv()
    r_own[...] = (
        q_own[pl.ds(pl.multiple_of(x * 32, 32), 32), :] + x_recv[0] + x_recv[1] + x_recv[2]
    )
    zr = send(
        r_own.at[pl.ds(pl.multiple_of((1 - zh) * 16, 16), 16), :],
        z_recv,
        s_z.at[1],
        r_z.at[1],
        zdev[4],
    )
    wx[1, 0].wait_recv()
    src = w_all.at[xs[3], halves[0], own_lane]
    wx_fwd = [send(src, src, s_x.at[19], r_x.at[19], xdev[1])]
    wx[3, 1].wait_recv()
    src = w_all.at[xs[1], halves[1], own_lane]
    wx_fwd.append(send(src, src, s_x.at[20], r_x.at[20], xdev[3]))

    zr.wait_recv()
    code_val = (r_own[pl.ds(pl.multiple_of(zh * 16, 16), 16), :] + z_recv[...]).astype(BF16)
    code_sh[...] = jnp.where(y == 3, jnp.zeros_like(code_val), code_val)
    cz = [
        send(code_sh, code.at[x, slab, own_half], s_z.at[2 + k], r_z.at[2 + k], updev[k])
        for k in range(8)
    ]
    wx[1, 1].wait_recv()
    core_out(xs[3], 4)
    wx[3, 0].wait_recv()
    core_out(xs[1], 5)
    for cp in ga_in:
        cp.wait_recv()
    l_ga.wait()
    gac = send(ga.at[c], ga.at[c], s_core.at[10], r_core.at[10], sib)
    for cp in wx_fwd:
        cp.wait_recv()
    core_out(xs[2], 6)
    for cp in wc:
        cp.wait_recv()

    gac.wait_recv()
    l_dec.wait()
    for j in range(4):
        lanes = pl.ds(j * 128, 128)
        g = jnp.concatenate(
            [ga[0, :, :, lanes].reshape(128, 128), ga[1, :, :, lanes].reshape(128, 128)], axis=1
        )
        part = lax.dot_general(g, w_all[j, own_half, :], LAST, preferred_element_type=F32)
        if j == 0:
            pb[...] = part
        else:
            pb[...] += part
    pb_s[...] = pb[...].astype(BF16).reshape(8, 16, 512)
    pr = []
    for k in range(1, 8):
        to_z = (z + k) % 8
        src = pb_s.at[(to_z % 4) * 2 + to_z // 4]
        pr.append(send(src, pb_r.at[k - 1], s_z.at[20 + k], r_z.at[20 + k], zdev[k]))

    for cp in cz:
        cp.wait_recv()
    cc = [to_sibling(code, x, 11)]
    cx = gather_x(code, 22)

    l_gain.wait()
    lane_id = lax.broadcasted_iota(jnp.int32, (128, 128), 1)
    ssq[...] = jnp.zeros_like(ssq)

    def scaled(k, dec, col, squares):
        cols = pl.ds(pl.multiple_of(col, 256), 256)
        normed[k, :, cols] = (dec * gain_v[:, cols]).astype(BF16)
        sq = dec * dec
        return squares + sq[:, :128] + sq[:, 128:]

    def add_squares(k, squares):
        total = jnp.sum(squares, axis=1, keepdims=True)
        ssq[...] += jnp.where(lane_id == k, total, 0.0).reshape(4, 32, 128)

    def near_half(k):
        slot = xs[(4 - k) % 4]
        cc[k].wait_recv()
        squares = jnp.zeros((128, 128), F32)
        for i in range(4):
            j = (2 * c + i) % 4
            dec = jnp.dot(code[slot], w_all[j], preferred_element_type=F32).astype(BF16)
            if k == 0 and i < 2:
                dec_s[:, pl.ds(i * 256, 256)] = dec
            if k == 0 and i == 1:
                dz.append(send(dec_s, dfar.at[x, :, own_half], s_z.at[0], r_z.at[0], zdev[4]))
            squares = scaled(k, dec.astype(F32), zh * 1024 + j * 256, squares)
        add_squares(k, squares)

    dz = []
    near_half(0)
    for cp in pr:
        cp.wait_recv()
    cg = pb[slab, :]
    for k in range(7):
        cg += pb_r[k].astype(F32)
    cg = cg.astype(BF16)
    cg_sh[...] = jnp.where(y == 0, jnp.zeros_like(cg), cg)
    rz = [
        send(cg_sh, ret.at[x, slab, own_half], s_z.at[28 + k], r_z.at[28 + k], downdev[k])
        for k in range(8)
    ]
    sz = [
        send(st_sh, st.at[x, slab, own_half], s_z.at[10 + k], r_z.at[10 + k], zdev[k])
        for k in range(1, 8)
    ]
    for k in range(1, 4):
        cx[k - 1].wait_recv()
        cc.append(to_sibling(code, xs[4 - k], 11 + k))
    for k in range(1, 4):
        near_half(k)
    dz[0].wait_recv()
    dc = [to_sibling(dfar, x, 23)]
    dx = gather_x(dfar, 32)

    for cp in l_gu:
        cp.wait()
    own_m = pl.ds(pl.multiple_of(dp * 32, 32), 32)

    is_end = ((dp + 1) // 2 + 1) % 2
    near = 1 + dp % 2
    other_dp = (dp * 3 + 2) % 5
    opp = 3 * (1 - dp // 2)
    third_dp = is_end * near + (1 - is_end) * opp
    third_slot = 1 + 2 * is_end
    far_m = pl.ds(pl.multiple_of(opp * 32, 32), 32)

    def at_dp(v):
        return (v, y, t)

    def r_in(k, h, slot):
        return r_gu.at[(k * 2 + h) * 4 + slot]

    def third(k, h):
        return pltpu.make_async_remote_copy(
            src_ref=gu_s.at[k, h, opp],
            dst_ref=gu_r.at[k, h, third_slot],
            send_sem=s_gu.at[(k * 2 + h) * 3 + 2],
            recv_sem=r_in(k, h, third_slot),
            device_id=at_dp(third_dp),
            device_id_type=MESH,
        )

    def wait_in(k, h, slot):
        ref = gu_r.at[k, h, slot]
        pltpu.make_async_remote_copy(
            src_ref=ref,
            dst_ref=ref,
            send_sem=s_gu.at[0],
            recv_sem=r_in(k, h, slot),
            device_id=dpdev[1],
            device_id_type=MESH,
        ).wait_recv()

    def group(k):
        slot = xs[(4 - k) % 4]
        dc[k].wait_recv()
        squares = jnp.zeros((128, 128), F32)
        for j in range(4):
            dec = dfar[slot, :, pl.ds(j * 256, 256)].astype(F32)
            squares = scaled(k, dec, (1 - zh) * 1024 + j * 256, squares)
        add_squares(k, squares)

        for h in range(2):
            v = jnp.dot(normed[k], wgu[h], preferred_element_type=F32)
            acc[...] = v
            gu_s[k, h] = v.astype(BF16).reshape(4, 32, 896)
            i = (k * 2 + h) * 3

            @pl.when(is_end == 1)
            def _():
                third(k, h).start()

            send(gu_s.at[k, h, near], gu_r.at[k, h, is_end], s_gu.at[i], r_in(k, h, is_end), at_dp(near))
            send(
                gu_s.at[k, h, other_dp],
                gu_r.at[k, h, 2 * is_end],
                s_gu.at[i + 1],
                r_in(k, h, 2 * is_end),
                at_dp(other_dp),
            )
            gu_own[k, h] = acc[own_m, :]
            gu_far[k, h] = acc[far_m, :]

    def merge(k):
        @pl.when(is_end == 0)
        def _():
            for h in range(2):
                wait_in(k, h, 3)
                gu_s[k, h, opp] = (gu_far[k, h] + gu_r[k, h, 3].astype(F32)).astype(BF16)
                third(k, h).start()

    group(0)
    for k in range(1, 4):
        dx[k - 1].wait_recv()
        dc.append(to_sibling(dfar, xs[4 - k], 23 + k))
    group(1)
    merge(0)
    for cp in rz:
        cp.wait_recv()
    rc = [to_sibling(ret, x, 19)]
    rx = gather_x(ret, 28)
    group(2)
    merge(1)
    group(3)
    sq_in = [
        send(ssq.at[(dp + q) % 4], ssq_r.at[q - 1], s_gu.at[23 + q], r_gu.at[31 + q], dpdev[q])
        for q in range(1, 4)
    ]
    for cp in sz:
        cp.wait_recv()
    sc = [to_sibling(st, x, 15)]
    sx = gather_x(st, 25)
    merge(2)
    merge(3)

    for k in range(1, 4):
        sx[k - 1].wait_recv()
        sc.append(to_sibling(st, xs[4 - k], 15 + k))
    l_grad.wait()
    for cp in sc:
        cp.wait_recv()
    grads = grad_v[...].reshape(4, 2, 4, 16, 128)
    perm = jnp.concatenate([grads[:, :, v].reshape(128, 128) for v in range(4)], axis=0)
    for h in range(4):
        cols = pl.ds(h * 256, 256)
        lhs = st[:, :, cols].reshape(512, 256)
        decg_o[0, cols, :] = lax.dot_general(lhs, perm, FIRST, preferred_element_type=F32)

    for k in range(1, 4):
        rx[k - 1].wait_recv()
        rc.append(to_sibling(ret, xs[4 - k], 19 + k))
    for cp in rc:
        cp.wait_recv()
    l_stin.wait()
    for cp in si:
        cp.wait_recv()
    for v in range(4):
        own_ret = ret[v, own_m, :]
        ing_o[0, pl.ds(v * 32, 32), :] = lax.dot_general(
            own_ret, enc_v[...], LAST, preferred_element_type=F32
        ).astype(BF16)
    rhs = ret[:, :, pl.ds(pl.multiple_of(dp * 256, 256), 256)].reshape(512, 256)
    for h in range(2):
        cols = pl.ds(h * 256, 256)
        lhs = jnp.concatenate(
            [stin_v[:, pl.ds(v * 32, 32), cols].reshape(128, 256) for v in range(4)], axis=0
        )
        encg_o[0, cols, :] = lax.dot_general(lhs, rhs, FIRST, preferred_element_type=F32)

    for cp in sq_in:
        cp.wait_recv()
    total = ssq[dp] + ssq_r[0] + ssq_r[1] + ssq_r[2]
    inv_all = lax.rsqrt(total / D + epsilon)
    for k in range(4):
        for h in range(2):
            wait_in(k, h, 0)
            wait_in(k, h, 1)

        @pl.when(is_end == 0)
        def _():
            for h in range(2):
                wait_in(k, h, 2)
                gu_own[k, h] += gu_r[k, h, 2].astype(F32)

        inv = inv_all[:, k : k + 1]
        rows = pl.ds(pl.multiple_of(xs[(4 - k) % 4] * 32, 32), 32)
        gate, up = [
            (gu_own[k, h] + gu_r[k, h, 0].astype(F32) + gu_r[k, h, 1].astype(F32)) * inv
            for h in range(2)
        ]
        act_o[0, rows, :] = (gate / (1.0 + jnp.exp(-gate)) * up).astype(BF16)

    for cp in pending:
        cp.wait_send()
    for k in range(4):
        for h in range(2):
            third(k, h).wait_send()


def hand_over(a, b, c, d, a_o, b_o, c_o, d_o, a_v, b_v, c_v, d_v, sem):
    steps = ((c, c_v, c_o), (d, d_v, d_o), (a, a_v, a_o), (b, b_v, b_o))
    loads = [pltpu.make_async_copy(src, via, sem.at[i]) for i, (src, via, _) in enumerate(steps)]
    stores = [
        pltpu.make_async_copy(via, dst, sem.at[4 + i]) for i, (_, via, dst) in enumerate(steps)
    ]
    for cp in loads:
        cp.start()
    for load, store in zip(loads, stores):
        load.wait()
        store.start()
    for cp in stores:
        cp.wait()


def per_device(
    outgoing,
    stashed_inputs,
    encoder,
    decoder,
    norm_gain,
    gate_matrix,
    up_matrix,
    grad_decoded,
    stashed_codes,
):
    grad = grad_decoded.reshape(4, 128, 128)
    anywhere = pl.BlockSpec(memory_space=pl.ANY)
    vmem = pl.BlockSpec(memory_space=pltpu.VMEM)
    V = pltpu.VMEM
    DMA = pltpu.SemaphoreType.DMA
    shapes = (
        jax.ShapeDtypeStruct((1, 128, 896), BF16),
        jax.ShapeDtypeStruct((1, 128, 512), BF16),
        jax.ShapeDtypeStruct((1, 512, 256), F32),
        jax.ShapeDtypeStruct((1, 1024, 128), F32),
    )
    results = pl.pallas_call(
        kernel,
        name="section",
        out_shape=shapes,
        in_specs=[anywhere] * 8 + [vmem],
        out_specs=(vmem,) * 4,
        scratch_shapes=[
            V((128, 512), BF16),
            V((512, 1024), BF16),
            V((1, 2048), F32),
            V((4, 128, 128), BF16),
            V((4, 128, 512), BF16),
            V((2, 2048, 896), BF16),
            V((4, 1024, 256), BF16),
            V((128, 512), F32),
            V((128, 512), F32),
            V((128, 512), F32),
            V((3, 32, 512), F32),
            V((32, 512), F32),
            V((16, 512), F32),
            V((16, 512), BF16),
            V((4, 128, 1024), BF16),
            V((16, 512), BF16),
            V((16, 512), BF16),
            V((16, 512), BF16),
            V((4, 128, 1024), BF16),
            V((2, 4, 32, 512), BF16),
            V((128, 512), F32),
            V((8, 16, 512), BF16),
            V((7, 16, 512), BF16),
            V((16, 512), BF16),
            V((4, 128, 1024), BF16),
            V((128, 512), BF16),
            V((4, 128, 1024), BF16),
            V((4, 128, 2048), BF16),
            V((128, 896), F32),
            V((4, 2, 4, 32, 896), BF16),
            V((4, 2, 4, 32, 896), BF16),
            V((4, 2, 32, 896), F32),
            V((4, 2, 32, 896), F32),
            V((4, 32, 128), F32),
            V((3, 32, 128), F32),
            DMA((7,)),
            DMA((2,)),
            DMA((27,)),
            DMA((27,)),
            DMA((36,)),
            DMA((36,)),
            DMA((36,)),
            DMA((36,)),
            DMA((27,)),
            DMA((35,)),
        ],
        compiler_params=pltpu.CompilerParams(
            collective_id=0, has_side_effects=True, vmem_limit_bytes=60 * 2**20
        ),
    )(
        outgoing,
        stashed_inputs,
        encoder,
        decoder,
        norm_gain,
        gate_matrix,
        up_matrix,
        grad,
        stashed_codes,
    )
    return pl.pallas_call(
        hand_over,
        name="hand_over",
        out_shape=shapes,
        in_specs=[anywhere] * 4,
        out_specs=(anywhere,) * 4,
        scratch_shapes=[V(s.shape, s.dtype) for s in shapes] + [DMA((8,))],
        compiler_params=pltpu.CompilerParams(vmem_limit_bytes=60 * 2**20),
    )(*results)


def solution(mesh):
    placed = (
        P("pipe", "dp", "tensor"),
        P("pipe", "dp", "tensor"),
        P("pipe", "tensor", None),
        P("pipe", None, ("dp", "tensor")),
        P("pipe", "dp"),
        P("pipe", "dp", "tensor"),
        P("pipe", "dp", "tensor"),
        P("pipe", None, ("dp", "tensor")),
        P("pipe", ("dp", "tensor"), None),
    )
    return jax.shard_map(
        per_device,
        mesh=mesh,
        in_specs=placed,
        out_specs=(
            P("pipe", "dp", "tensor"),
            P("pipe", "dp", "tensor"),
            P("pipe", "tensor", "dp"),
            P("pipe", None, ("dp", "tensor")),
        ),
        check_vma=False,
    )
```

time: 90.3 us -> 87.2 us (0.966)
  Pallas kernels: 89.5 us -> 86.4 us
    pallas_call x1, Pallas kernels: 87.3 us -> 84.2 us  [per_device(): pl.pallas_call(kernel, name='section', out_shape=shapes, in_specs=[anywhe...]
where the time goes in v3:
time: 87.2 us; the launch traced here: 87 us
  Pallas kernels  86.4 us (99%)
    pallas_call x1, Pallas kernels, per_device(): pl.pallas_call(kernel, name='section', out_shape=shapes, in_specs=[anywhe...  84.2 us
    pallas_call x1, Pallas kernels, per_device(): pl.pallas_call(hand_over, name='hand_over', out_shape=shapes, in_specs=[a...  2.19 us

profile of v3, /device:TPU:1, one launch (start us, length us, event | category | flops | bytes accessed | tf_op | source)
XLA Modules:
  0.0 87.0 jit_solution(5509450883355929907)
XLA Ops:
  0.6 84.2 %section.1 = (bf16[1,128,896]{2,1,0:T(8,128)(2,1)}, bf16[1,128,512]{2,1,0:T(8,128)(2,1)}, f32[1,512,256]{2,1,0:T(8,128)}, f32[1,1024,128]{2,1,0:T(8,128)}) custom-call(bf16[1,128,512]{2,1,0:T(8,128)(2,1)} %out_h.1, bf16[1,128,512]{2,1,0:T(8,128)(2,1)} %stin_h.1, bf16[1,512,1024]{2,1,0:T(8,128)(2,1)} %enc_h.1, bf16[1,1024,128]{2,1,0:T(8,128)(2,1)} %dec_h.1, ...), custom_call_target="tpu_custom_call" | custom-call | tf_op jit(solution)/shard_map/section/pallas_call | solution.py:521
  84.8 2.2 %hand_over.1 = (bf16[1,128,896]{2,1,0:T(8,128)(2,1)}, bf16[1,128,512]{2,1,0:T(8,128)(2,1)}, f32[1,512,256]{2,1,0:T(8,128)}, f32[1,1024,128]{2,1,0:T(8,128)}) custom-call(bf16[1,128,896]{2,1,0:T(8,128)(2,1)} %get-tuple-element.8.a, bf16[1,128,512]{2,1,0:T(8,128)(2,1)} %get-tuple-element.9.b, f32[1,512,256]{2,1,0:T(8,128)} %get-tuple-element.10.c, ...), custom_call_target="tpu_custom_call" | custom-call | tf_op jit(solution)/shard_map/hand_over/pallas_call | solution.py:588

commit v4 on v3

--- a/solution.py
+++ b/solution.py
@@ -63,6 +63,7 @@
     gu_own,
     gu_far,
     ssq,
+    ssq_row,
     ssq_r,
     local_sem,
     wload_sem,
@@ -403,17 +404,18 @@
         cp.wait_recv()
     rc = [to_sibling(ret, x, 19)]
     rx = gather_x(ret, 28)
+    for cp in sz:
+        cp.wait_recv()
+    sc = [to_sibling(st, x, 15)]
+    sx = gather_x(st, 25)
     group(2)
     merge(1)
     group(3)
+    ssq_row[...] = ssq[...].reshape(128, 128).T[:8]
     sq_in = [
-        send(ssq.at[(dp + q) % 4], ssq_r.at[q - 1], s_gu.at[23 + q], r_gu.at[31 + q], dpdev[q])
+        send(ssq_row, ssq_r.at[q - 1], s_gu.at[23 + q], r_gu.at[31 + q], dpdev[q])
         for q in range(1, 4)
     ]
-    for cp in sz:
-        cp.wait_recv()
-    sc = [to_sibling(st, x, 15)]
-    sx = gather_x(st, 25)
     merge(2)
     merge(3)
 
@@ -453,8 +455,10 @@
 
     for cp in sq_in:
         cp.wait_recv()
-    total = ssq[dp] + ssq_r[0] + ssq_r[1] + ssq_r[2]
-    inv_all = lax.rsqrt(total / D + epsilon)
+    total = ssq_row[...] + ssq_r[0] + ssq_r[1] + ssq_r[2]
+    total = jnp.concatenate([total, jnp.zeros((120, 128), F32)], axis=0)
+    ssq[...] = total.T.reshape(4, 32, 128)
+    inv_all = lax.rsqrt(ssq[dp] / D + epsilon)
     for k in range(4):
         for h in range(2):
             wait_in(k, h, 0)
@@ -559,7 +563,8 @@
             V((4, 2, 32, 896), F32),
             V((4, 2, 32, 896), F32),
             V((4, 32, 128), F32),
-            V((3, 32, 128), F32),
+            V((8, 128), F32),
+            V((3, 8, 128), F32),
             DMA((7,)),
             DMA((2,)),
             DMA((27,)),

time: 87.2 us -> 86.1 us (0.987)
  Pallas kernels: 86.4 us -> 85.3 us
    pallas_call x1, Pallas kernels: 84.2 us -> 83.2 us  [per_device(): pl.pallas_call(kernel, name='section', out_shape=shapes, in_specs=[anywhe...]
where the time goes in v4:
time: 86.1 us; the launch traced here: 86 us
  Pallas kernels  85.3 us (99%)
    pallas_call x1, Pallas kernels, per_device(): pl.pallas_call(kernel, name='section', out_shape=shapes, in_specs=[anywhe...  83.2 us
    pallas_call x1, Pallas kernels, per_device(): pl.pallas_call(hand_over, name='hand_over', out_shape=shapes, in_specs=[a...  2.19 us

profile of v4, /device:TPU:1, one launch (start us, length us, event | category | flops | bytes accessed | tf_op | source)
XLA Modules:
  0.0 86.0 jit_solution(5854471918553857168)
XLA Ops:
  0.6 83.2 %section.1 = (bf16[1,128,896]{2,1,0:T(8,128)(2,1)}, bf16[1,128,512]{2,1,0:T(8,128)(2,1)}, f32[1,512,256]{2,1,0:T(8,128)}, f32[1,1024,128]{2,1,0:T(8,128)}) custom-call(bf16[1,128,512]{2,1,0:T(8,128)(2,1)} %out_h.1, bf16[1,128,512]{2,1,0:T(8,128)(2,1)} %stin_h.1, bf16[1,512,1024]{2,1,0:T(8,128)(2,1)} %enc_h.1, bf16[1,1024,128]{2,1,0:T(8,128)(2,1)} %dec_h.1, ...), custom_call_target="tpu_custom_call" | custom-call | tf_op jit(solution)/shard_map/section/pallas_call | solution.py:525
  83.8 2.2 %hand_over.1 = (bf16[1,128,896]{2,1,0:T(8,128)(2,1)}, bf16[1,128,512]{2,1,0:T(8,128)(2,1)}, f32[1,512,256]{2,1,0:T(8,128)}, f32[1,1024,128]{2,1,0:T(8,128)}) custom-call(bf16[1,128,896]{2,1,0:T(8,128)(2,1)} %get-tuple-element.8.a, bf16[1,128,512]{2,1,0:T(8,128)(2,1)} %get-tuple-element.9.b, f32[1,512,256]{2,1,0:T(8,128)} %get-tuple-element.10.c, ...), custom_call_target="tpu_custom_call" | custom-call | tf_op jit(solution)/shard_map/hand_over/pallas_call | solution.py:593
